TPU v7x, 32 devices: a whole 2x2x4 slice. The times are simulated.
32 devices in a mesh: groups: 2 (over y), dp: 4 (over z), tensor: 2 (over x), sub: 2 (over core).
Axes of the slice: x: 2, y: 2, z: 4, core: 2. Of those that a mesh axis runs over, the one named last changes fastest.
Arguments:
- acts: bfloat16 [2, 8192, 14336], P(None, ('groups', 'dp'), ('tensor', 'sub')), parts along dimension 1, may hold values from -6 to 6
- grads_out: bfloat16 [2, 8192, 4096], P(None, ('groups', 'dp'), ('tensor', 'sub')), parts along dimension 1, may hold values from -6 to 6
- lengths: int32 [16], P(('groups', 'dp')), parts along dimension 0, may hold values from 128 to 512
- proj_in: bfloat16 [2, 14336, 64], P(None, ('tensor', 'sub')), may hold values from -0.046875 to 0.046875
- proj_out: bfloat16 [2, 4096, 64], P(None, ('tensor', 'sub')), may hold values from -0.09375 to 0.09375
- query_grads: bfloat16 [256, 8192], P('dp', ('tensor', 'sub')), may hold values from -0.0625 to 0.0625
Outputs:
- sketches: float32 [16, 8192], P(('groups', 'dp'), ('tensor', 'sub')), parts along dimension 0
- scores: float32 [256, 16], P(None, ('groups', 'dp')), parts along dimension 1
There are 2 independent parts, one for each index of `groups`. A program takes and returns all parts, laid end to end along the dimension named above; an argument that names none is the same for every part. Nothing has to cross between parts.
Inputs may be any that keep to these rules, and one draw needn't show every extreme that they name: The live tokens of a sequence are its first lengths[e] slots.
All inputs are finite; a program needn't handle non-finite values.
Results may differ from a plain program's by a relative error of at most 0.0003.
Values may be sent and summed in bfloat16 or wider, within the bound.
A program may use at most 64 MiB of HBM per device.

v0:
```python
import jax
import jax.numpy as jnp
from jax import lax
from jax.sharding import PartitionSpec as P

SEQ_LEN = 512


def project_side(inputs, weights):
    return jnp.concatenate(
        [
            jnp.dot(inputs[layer], weights[layer], preferred_element_type=jnp.float32)
            for layer in range(inputs.shape[0])
        ],
        axis=1,
    )


def sketch_terms(side_a, side_b, weights, layers):
    rows = side_a.shape[0]
    width = side_a.shape[1] // layers
    left = side_a.reshape(rows, layers, width)
    right = side_b.reshape(rows, layers, width)
    result = jnp.einsum("te,tli,tlj->elij", weights, left, right, precision=lax.Precision.HIGHEST)
    return (result * SEQ_LEN ** (-0.5)).reshape(weights.shape[1], layers * width * width)


def row_weights(lengths, rows, seq_len):
    token = jnp.arange(rows, dtype=jnp.int32)
    seq_of = token // seq_len
    slot = token % seq_len
    owners = jnp.arange(lengths.shape[0], dtype=jnp.int32)
    match = seq_of[:, None] == owners[None, :]
    bound = jnp.sum(jnp.where(match, lengths[None, :], 0), axis=1)
    live = (slot < bound).astype(jnp.float32)
    return match.astype(jnp.float32) * live[:, None]


def per_device(acts, grads_out, lengths, proj_in, proj_out, query_grads):
    layers, rows, _ = acts.shape
    seqs = lengths.shape[0]
    seq_len = rows // seqs
    side_a = project_side(acts, proj_in)
    side_b = project_side(grads_out, proj_out)
    count = lax.axis_size(("tensor", "sub"))
    rank = lax.axis_index(("tensor", "sub"))
    feats = layers * proj_in.shape[2] * proj_in.shape[2]
    share = feats // count
    whole_a, whole_b = lax.psum((side_a, side_b), ("tensor", "sub"))
    weights = row_weights(lengths, rows, seq_len)
    full_sketch = sketch_terms(whole_a, whole_b, weights, layers)
    mine = lax.dynamic_slice_in_dim(full_sketch, rank * share, share, 1)
    block = jnp.dot(
        lax.all_gather(query_grads, "dp", axis=0, tiled=True).astype(jnp.float32),
        mine.T,
        precision=lax.Precision.HIGHEST,
    )
    scores = lax.psum(block, ("tensor", "sub"))
    return (mine, scores)


def solution(mesh):
    placed = (
        P(None, ("groups", "dp"), ("tensor", "sub")),
        P(None, ("groups", "dp"), ("tensor", "sub")),
        P(("groups", "dp")),
        P(None, ("tensor", "sub"), None),
        P(None, ("tensor", "sub"), None),
        P("dp", ("tensor", "sub")),
    )
    return jax.shard_map(
        per_device,
        mesh=mesh,
        in_specs=placed,
        out_specs=(P(("groups", "dp"), ("tensor", "sub")), P(None, ("groups", "dp"))),
        check_vma=False,
    )
```

profile of v0, /device:TPU:0, one launch (start us, length us, event | category | flops | bytes accessed | tf_op | source)
XLA Modules:
  0.0 81.2 jit_solution(12404867172954028309)
XLA Ops:
  8.0 0.0 all-reduce.3.cloned.1.call-start
  8.0 2.4 %fusion.6 = f32[1024,64]{0,1:T(8,128)S(1)} fusion(bf16[2,1024,1024]{2,1,0:T(8,128)(2,1)} %param.7, bf16[2,1024,64]{1,2,0:T(8,128)(2,1)} %param.10), kind=kOutput, calls=%fused_computation.6 | convolution fusion | flops 134217728 | bytes 2490368 | tf_op jit(solution)/shard_map/dot_general | solution.py:12
  10.4 0.0 copy-start.2
  10.4 2.5 %fusion.8 = f32[1024,64]{0,1:T(8,128)S(1)} fusion(bf16[2,1024,1024]{2,1,0:T(8,128)(2,1)} %param.7, bf16[2,1024,64]{1,2,0:T(8,128)(2,1)} %param.10), kind=kOutput, calls=%fused_computation.8 | convolution fusion | flops 134217728 | bytes 2490368 | tf_op jit(solution)/shard_map/dot_general | solution.py:12
  12.9 0.0 copy-start.3
  12.9 6.2 %fusion = f32[1024,64]{0,1:T(8,128)S(1)} fusion(bf16[2,1024,3584]{2,1,0:T(8,128)(2,1)} %param.6, bf16[2,3584,64]{1,2,0:T(8,128)(2,1)} %param.9), kind=kOutput, calls=%fused_computation | convolution fusion | flops 469762048 | bytes 8060928 | tf_op jit(solution)/shard_map/dot_general | solution.py:12
  19.1 0.0 copy-done.2
  19.1 0.0 copy-done.3
  19.1 0.0 copy-start.1
  19.1 2.3 %fusion.2 = f32[1024,64]{0,1:T(8,128)S(1)} fusion(bf16[2,1024,3584]{2,1,0:T(8,128)(2,1)S(1)} %copy-done.2, bf16[2,3584,64]{1,2,0:T(8,128)(2,1)S(1)} %copy-done.3), kind=kOutput, calls=%fused_computation.2 | convolution fusion | flops 469762048 | bytes 8060928 | tf_op jit(solution)/shard_map/dot_general | solution.py:12
  21.5 0.8 %pad_maximum_fusion.1 = f32[1024,128]{0,1:T(8,128)} fusion(f32[1024,64]{0,1:T(8,128)S(1)} %fusion.6, f32[1024,64]{0,1:T(8,128)S(1)} %fusion.8), kind=kLoop, calls=%fused_computation.17 | loop fusion | flops 131072 | bytes 1048576 | tf_op jit(solution)/shard_map/concatenate | solution.py:10
  22.3 0.8 %pad_maximum_fusion = f32[1024,128]{0,1:T(8,128)} fusion(f32[1024,64]{0,1:T(8,128)S(1)} %fusion, f32[1024,64]{0,1:T(8,128)S(1)} %fusion.2), kind=kLoop, calls=%fused_computation.16 | loop fusion | flops 131072 | bytes 1048576 | tf_op jit(solution)/shard_map/concatenate | solution.py:10
  23.1 0.0 all-reduce.3.cloned.1.call-update
  23.2 0.0 all-gather.2.cloned.1.call-start
  23.2 0.5 all-gather.2.cloned.1.call-update
  23.8 0.0 copy-done.1
  23.8 0.1 select_reduce_fusion
  23.9 38.4 %all-reduce.3.cloned.1.call-done = (f32[1024,2,64]{0,2,1:T(8,128)}, f32[1024,2,64]{0,2,1:T(8,128)}) async-done(((f32[1024,2,64]{0,2,1:T(8,128)}, f32[1024,2,64]{0,2,1:T(8,128)}), (f32[1024,2,64]{0,2,1:T(8,128)}, f32[1024,2,64]{0,2,1:T(8,128)})) %all-reduce.3.cloned.1.call-update) | async-done | bytes 1048592 | tf_op jit(solution)/shard_map/psum | solution.py:49
  62.3 2.3 %fusion.12 = f32[2,2,64,64]{3,2,0,1:T(8,128)S(1)} fusion(f32[1024,2,64]{0,2,1:T(8,128)} %get-tuple-element.2, f32[1024,2]{0,1:T(2,128)S(1)} %fusion.25, f32[1024,2,64]{0,2,1:T(8,128)} %get-tuple-element.3), kind=kOutput, calls=%fused_computation.13 | convolution fusion | flops 201605120 | bytes 1122304 | tf_op jit(solution)/shard_map/te,tli,tlj->elij/dot_general | solution.py:24
  64.6 0.1 reshape.42
  64.7 0.0 copy-start
  64.7 0.0 all-gather.2.cloned.1.call-done
  64.7 2.1 %convolution_bitcast_fusion = f32[256,2]{0,1:T(2,128)S(1)} fusion(f32[2,2048]{1,0:T(2,128)S(1)} %constant_dynamic-slice_fusion, bf16[256,2048]{1,0:T(8,128)(2,1)} %all-gather.2.cloned.1.call-done), kind=kOutput, calls=%fused_computation.14 | convolution fusion | flops 12582912 | bytes 1067008 | tf_op jit(solution)/shard_map/dot_general | solution.py:53
  66.9 6.8 %psum.23 = f32[256,2]{0,1:T(2,128)} all-reduce(f32[256,2]{0,1:T(2,128)S(1)} %convolution_bitcast_fusion), channel_id=1, replica_groups=mesh['groups'=2,'dp'=4,'tensor'=2,'sub'=2] {'tensor','sub'}, use_global_device_ids=true, to_apply=%region_3.4 | all-reduce | flops 512 | bytes 4096 | tf_op jit(solution)/shard_map/psum | solution.py:58
  73.7 0.0 copy-done
  (5 shorter events, 0.0 us)
Async XLA Ops:
  8.0 54.3 %all-reduce.3.cloned.1.call-start = ((), (), s32[]{:S(2)}) async-start(), calls=%async_computation.1 | async-start | bytes 2097152 | tf_op jit(solution)/shard_map/psum | solution.py:49
  10.4 8.7 %copy-start.2 = (bf16[2,1024,3584]{2,1,0:T(8,128)(2,1)S(1)}, bf16[2,1024,3584]{2,1,0:T(8,128)(2,1)}, u32[]{:S(2)}) copy-start(bf16[2,1024,3584]{2,1,0:T(8,128)(2,1)} %param.6) | copy-start | bytes 44040196
  12.9 6.2 %copy-start.3 = (bf16[2,3584,64]{1,2,0:T(8,128)(2,1)S(1)}, bf16[2,3584,64]{1,2,0:T(8,128)(2,1)}, u32[]{:S(2)}) copy-start(bf16[2,3584,64]{1,2,0:T(8,128)(2,1)} %param.9) | copy-start | bytes 2752516
  19.1 4.6 %copy-start.1 = (s32[2]{0:T(128)S(1)}, s32[2]{0:T(128)}, u32[]{:S(2)}) copy-start(s32[2]{0:T(128)} %param.8) | copy-start | bytes 28
  23.2 41.6 %all-gather.2.cloned.1.call-start = ((), (), s32[]{:S(2)}) async-start(), calls=%async_computation | async-start | bytes 1310720 | tf_op jit(solution)/shard_map/all_gather | solution.py:54
  64.7 9.0 %copy-start = (f32[2,2048]{1,0:T(2,128)}, f32[2,2048]{1,0:T(2,128)S(1)}, u32[]{:S(2)}) copy-start(f32[2,2048]{1,0:T(2,128)S(1)} %constant_dynamic-slice_fusion) | copy-start | bytes 49156
Sparse Core Ops, SparseCore 0:
  23.3 38.9 all-reduce.2
Sparse Core Ops, SparseCore 1:
  25.3 30.5 all-gather.1
where the time goes:
time: 81.4 us; the launch traced here: 81.2 us
  waiting for transfers between devices  38.9 us (48%)
  matrix products  17.7 us (22%)
  between operations  15.6 us (19%)
  blocking collectives  6.85 us (8%)
  other arithmetic  1.79 us (2%)
    psum x1, waiting for transfers between devices, per_device(): whole_a, whole_b = lax.psum((side_a, side_b), ('tensor', 'sub'))  38.4 us
    dot_general x4, matrix products, project_side(): jnp.dot(inputs[layer], weights[layer], preferred_element_type=jnp.float32)  13.4 us
    psum x1, blocking collectives, per_device(): scores = lax.psum(block, ('tensor', 'sub'))  6.85 us
    dot_general x1, matrix products, sketch_terms(): jnp.einsum('te,tli,tlj->elij', weights, left, right, precision=lax.Precis...  2.26 us
    dot_general x1, matrix products, per_device(): jnp.dot(lax.all_gather(query_grads, 'dp', axis=0, tiled=True).astype(jnp....  2.14 us
    concatenate x2, other arithmetic, project_side(): jnp.concatenate([jnp.dot(inputs[layer], weights[layer], preferred_element...  1.69 us
  transfers between devices with their start and end apart: 2, of which 1 were waited for; matrix products, arithmetic and copies ran while one was open for 3% of the time, Pallas kernels for 0%

commit v1 on v0

--- a/solution.py
+++ b/solution.py
@@ -1,9 +1,15 @@
+import functools
 import jax
 import jax.numpy as jnp
 from jax import lax
+from jax.experimental import pallas as pl
+from jax.experimental.pallas import tpu as pltpu
 from jax.sharding import PartitionSpec as P
 
 SEQ_LEN = 512
+LANES = 128
+MESH = pl.DeviceIdType.MESH
+NT = (((1,), (1,)), ((), ()))
 
 
 def project_side(inputs, weights):
@@ -59,6 +65,239 @@
     return (mine, scores)
 
 
+def kernel(
+    dps, chunk, steps,
+    x_hbm, g_hbm, len_ref, w_hbm, v_hbm, q_hbm,
+    sk_ref, sc_ref,
+    x, g, w, v, q, away, mine, sub_in, ten_in, tab, flat_ref, all_sk, wide, snd, rcv,
+    x_sem, g_sem, w_sem, v_sem, q_sem,
+    sub_s, sub_r, ten_s, ten_r, sk_s, sk_r, sc_s, sc_r,
+):
+    d = lax.axis_index("dp")
+    t = lax.axis_index("tensor")
+    c = lax.axis_index("sub")
+    ot, oc = 1 - t, 1 - c
+    k = w.shape[1]
+    seq_len = SEQ_LEN
+
+    items = []
+    for layer in (ot, t):
+        for part in range(steps):
+            for half in (oc, c):
+                items.append((layer, half * seq_len + part * chunk))
+
+    def fetch_w(n, layer):
+        return (
+            pltpu.make_async_copy(w_hbm.at[layer], w.at[layer], w_sem.at[n]),
+            pltpu.make_async_copy(v_hbm.at[layer], v.at[layer], v_sem.at[n]),
+        )
+
+    def fetch(n):
+        layer, row = items[n]
+        at = pl.ds(pl.multiple_of(row, chunk), chunk)
+        return (
+            pltpu.make_async_copy(x_hbm.at[layer, at], x.at[layer, at], x_sem.at[n]),
+            pltpu.make_async_copy(g_hbm.at[layer, at], g.at[layer, at], g_sem.at[n]),
+        )
+
+    loads = []
+    weight_loads = [fetch_w(0, ot), fetch_w(1, t)]
+    for n in range(len(items)):
+        if n == 0 or n == len(items) // 2:
+            for copy in weight_loads[0 if n == 0 else 1]:
+                copy.start()
+        loads.append(fetch(n))
+        for copy in loads[-1]:
+            copy.start()
+    q_load = pltpu.make_async_copy(q_hbm, q, q_sem)
+    q_load.start()
+
+    others = []
+    for a in range(dps):
+        for b in range(2):
+            for e in range(2):
+                if a or b or e:
+                    others.append((lax.rem(d + a, dps), lax.rem(t + b, 2), lax.rem(c + e, 2)))
+    barrier = pltpu.get_barrier_semaphore()
+    for dd, tt, cc in others:
+        pl.semaphore_signal(
+            barrier, inc=1, device_id={"dp": dd, "tensor": tt, "sub": cc}, device_id_type=MESH
+        )
+
+    def project(n, out):
+        if n == 0 or n == len(items) // 2:
+            for copy in weight_loads[0 if n == 0 else 1]:
+                copy.wait()
+        for copy in loads[n]:
+            copy.wait()
+        layer, row = items[n]
+        at = pl.ds(pl.multiple_of(row, chunk), chunk)
+        out[:, 0:k] = lax.dot_general(x[layer, at, :], w[layer], NT, preferred_element_type=jnp.float32)
+        out[:, k : 2 * k] = lax.dot_general(g[layer, at, :], v[layer], NT, preferred_element_type=jnp.float32)
+
+    sub_copies, ten_copies = [], []
+    for s in range(2 * steps):
+        project(2 * s, away.at[s])
+        if s == 0:
+            pl.semaphore_wait(barrier, len(others))
+        copy = pltpu.make_async_remote_copy(
+            src_ref=away.at[s], dst_ref=sub_in.at[s], send_sem=sub_s.at[s], recv_sem=sub_r.at[s],
+            device_id={"sub": oc}, device_id_type=MESH,
+        )
+        copy.start()
+        sub_copies.append(copy)
+        project(2 * s + 1, mine.at[s])
+        copy.wait_recv()
+        mine[s] += sub_in[s]
+        if s < steps:
+            copy = pltpu.make_async_remote_copy(
+                src_ref=mine.at[s], dst_ref=ten_in.at[s], send_sem=ten_s.at[s], recv_sem=ten_r.at[s],
+                device_id={"tensor": ot}, device_id_type=MESH,
+            )
+            copy.start()
+            ten_copies.append(copy)
+
+    bound = len_ref[c]
+    lane = lax.broadcasted_iota(jnp.int32, (chunk, LANES), 1)
+    slot = lax.broadcasted_iota(jnp.int32, (chunk, LANES), 0)
+    total = jnp.zeros((LANES, LANES), jnp.float32)
+    for part in range(steps):
+        ten_copies[part].wait_recv()
+        both = mine[steps + part] + ten_in[part]
+        live = jnp.where(slot + part * chunk < bound, both, 0.0)
+        right = jnp.where(lane < k, pltpu.roll(both, k, 1), both)
+        total += jnp.dot(
+            live.T, right, precision=lax.Precision.HIGHEST, preferred_element_type=jnp.float32
+        )
+    tab[...] = total[0:k] * (seq_len ** -0.5)
+    pairs = k // 2
+    even = tab[pl.ds(0, pairs, stride=2), :]
+    odd = tab[pl.ds(1, pairs, stride=2), :]
+    lane2 = lax.broadcasted_iota(jnp.int32, (pairs, LANES), 1)
+    flat = jnp.where(lane2 < k, even, odd)
+    half = pairs // 2
+    flat_ref[0] = flat[0:half]
+    flat_ref[1] = flat[half:pairs]
+
+    def sk_copy(to_d, to_c, from_d, from_c, a, e):
+        return pltpu.make_async_remote_copy(
+            src_ref=flat_ref.at[to_c],
+            dst_ref=all_sk.at[pl.ds(pl.multiple_of((from_d * 2 + from_c) * half, half), half)],
+            send_sem=sk_s.at[a * 2 + e], recv_sem=sk_r.at[from_d * 2 + from_c],
+            device_id={"dp": to_d, "sub": to_c}, device_id_type=MESH,
+        )
+
+    pairs_ae = [(a, e) for a in reversed(range(dps)) for e in range(2) if a or e]
+    sk_copies = []
+    for a, e in pairs_ae:
+        copy = sk_copy(lax.rem(d + a, dps), lax.rem(c + e, 2), d, c, a, e)
+        copy.start()
+        sk_copies.append(copy)
+    all_sk[pl.ds(pl.multiple_of((d * 2 + c) * half, half), half)] = flat_ref[c]
+    q_load.wait()
+    for a, e in reversed(pairs_ae):
+        fd, fc = lax.rem(d + dps - a, dps), lax.rem(c + e, 2)
+        sk_copy(fd, fc, fd, fc, a, e).wait_recv()
+
+    seqs = 2 * dps
+    for m in range(half):
+        at = slice(m * LANES, (m + 1) * LANES)
+        value = all_sk[pl.ds(m, seqs, stride=half), :]
+        first = value.astype(jnp.bfloat16).astype(jnp.float32)
+        rest = value - first
+        second = rest.astype(jnp.bfloat16).astype(jnp.float32)
+        wide[0:seqs, at] = first
+        wide[seqs : 2 * seqs, at] = second
+        wide[2 * seqs : 3 * seqs, at] = rest - second
+        wide[3 * seqs : 4 * seqs, at] = jnp.zeros_like(value)
+    prod = lax.dot_general(
+        wide[...].astype(jnp.bfloat16), q[...], NT,
+        preferred_element_type=jnp.float32,
+    )
+    part = prod[0:seqs] + prod[seqs : 2 * seqs] + prod[2 * seqs : 3 * seqs]
+    rows_q = q.shape[0]
+    snd[...] = jnp.zeros_like(snd)
+    for to in range(dps):
+        snd[to, 0:2, 0:rows_q] = part[2 * to : 2 * to + 2]
+
+    def sc_copy(n, to, sender):
+        dd, tt, cc = to
+        fd, ft, fc = sender
+        slot_of = fd * 4 + ft * 2 + fc
+        return pltpu.make_async_remote_copy(
+            src_ref=snd.at[dd], dst_ref=rcv.at[slot_of],
+            send_sem=sc_s.at[n], recv_sem=sc_r.at[slot_of],
+            device_id={"dp": dd, "tensor": tt, "sub": cc}, device_id_type=MESH,
+        )
+
+    sc_copies = []
+    for n, to in enumerate(reversed(others)):
+        copy = sc_copy(n, to, (d, t, c))
+        copy.start()
+        sc_copies.append(copy)
+    rcv[d * 4 + t * 2 + c] = snd[d]
+
+    for e in range(2):
+        mine_sk = all_sk[pl.ds(pl.multiple_of((d * 2 + e) * half, half), half), :]
+        for m in range(half):
+            sk_ref[e : e + 1, m * LANES : (m + 1) * LANES] = mine_sk[m : m + 1, :]
+
+    for n, sender in enumerate(others):
+        sc_copy(n, sender, sender).wait_recv()
+    for dd in range(dps):
+        acc = (rcv[dd * 4] + rcv[dd * 4 + 1]) + (rcv[dd * 4 + 2] + rcv[dd * 4 + 3])
+        sc_ref[:, dd * rows_q : (dd + 1) * rows_q] = acc[0:2, 0:rows_q]
+    for copy in sub_copies + ten_copies + sk_copies + sc_copies:
+        copy.wait_send()
+
+
+def fused(dps, acts, grads_out, lengths, proj_in, proj_out, query_grads):
+    layers, rows, hidden = acts.shape
+    model = grads_out.shape[2]
+    k = proj_in.shape[2]
+    steps = 2
+    chunk = SEQ_LEN // steps
+    queries, share = query_grads.shape
+    half = share // LANES
+    ranks = dps * 4
+    f32, bf16 = jnp.float32, jnp.bfloat16
+    anywhere = pl.BlockSpec(memory_space=pltpu.HBM)
+    dma = pltpu.SemaphoreType.DMA
+    sketches, scores = pl.pallas_call(
+        functools.partial(kernel, dps, chunk, steps),
+        out_shape=(
+            jax.ShapeDtypeStruct((2, share), f32),
+            jax.ShapeDtypeStruct((2, dps * queries), f32),
+        ),
+        in_specs=[anywhere, anywhere, pl.BlockSpec(memory_space=pltpu.SMEM), anywhere, anywhere, anywhere],
+        out_specs=(pl.BlockSpec(memory_space=pltpu.VMEM), pl.BlockSpec(memory_space=pltpu.VMEM)),
+        scratch_shapes=[
+            pltpu.VMEM((layers, rows, hidden), bf16),
+            pltpu.VMEM((layers, rows, model), bf16),
+            pltpu.VMEM((layers, k, hidden), bf16),
+            pltpu.VMEM((layers, k, model), bf16),
+            pltpu.VMEM((queries, share), bf16),
+            pltpu.VMEM((2 * steps, chunk, LANES), f32),
+            pltpu.VMEM((2 * steps, chunk, LANES), f32),
+            pltpu.VMEM((2 * steps, chunk, LANES), f32),
+            pltpu.VMEM((steps, chunk, LANES), f32),
+            pltpu.VMEM((k, LANES), f32),
+            pltpu.VMEM((2, half, LANES), f32),
+            pltpu.VMEM((2 * dps * half, LANES), f32),
+            pltpu.VMEM((8 * dps, share), f32),
+            pltpu.VMEM((dps, 8, LANES), f32),
+            pltpu.VMEM((ranks, 8, LANES), f32),
+            dma((4 * steps,)), dma((4 * steps,)), dma((2,)), dma((2,)), dma,
+            dma((2 * steps,)), dma((2 * steps,)), dma((steps,)), dma((steps,)),
+            dma((2 * dps,)), dma((2 * dps,)), dma((ranks,)), dma((ranks,)),
+        ],
+        compiler_params=pltpu.CompilerParams(
+            collective_id=0, has_side_effects=True, vmem_limit_bytes=60 * 1024 * 1024
+        ),
+    )(acts, grads_out, lengths, proj_in.swapaxes(1, 2), proj_out.swapaxes(1, 2), query_grads)
+    return sketches, scores.T
+
+
 def solution(mesh):
     placed = (
         P(None, ("groups", "dp"), ("tensor", "sub")),
@@ -68,8 +307,24 @@
         P(None, ("tensor", "sub"), None),
         P("dp", ("tensor", "sub")),
     )
+
+    def body(acts, grads_out, lengths, proj_in, proj_out, query_grads):
+        layers, rows, _ = acts.shape
+        fits = (
+            mesh.shape["tensor"] == 2
+            and mesh.shape["sub"] == 2
+            and layers == 2
+            and lengths.shape[0] == 2
+            and rows == 2 * SEQ_LEN
+            and 2 * proj_in.shape[2] == LANES
+            and query_grads.shape[0] <= LANES
+            and 2 * mesh.shape["dp"] == 8
+        )
+        plan = functools.partial(fused, mesh.shape["dp"]) if fits else per_device
+        return plan(acts, grads_out, lengths, proj_in, proj_out, query_grads)
+
     return jax.shard_map(
-        per_device,
+        body,
         mesh=mesh,
         in_specs=placed,
         out_specs=(P(("groups", "dp"), ("tensor", "sub")), P(None, ("groups", "dp"))),

time: 81.4 us -> 31.4 us (0.39)
  waiting for transfers between devices: 38.9 us -> 0 us
  Pallas kernels: 0 us -> 28 us
  matrix products: 17.7 us -> 0 us
  between operations: 15.6 us -> 0.64 us
  blocking collectives: 6.85 us -> 0 us
  local copies, waits for them, and re-layouts: 0.16 us -> 2.55 us
  other arithmetic: 1.79 us -> 0 us
    psum x1 -> x0, waiting for transfers between devices: 38.4 us -> none  [per_device(): whole_a, whole_b = lax.psum((side_a, side_b), ('tensor', 'sub'))]
    pallas_call x0 -> x1, Pallas kernels: none -> 28 us  [fused(): pl.pallas_call(functools.partial(kernel, dps, chunk, steps), out_shape=(j...]
    dot_general x6 -> x0, matrix products: 17.7 us -> none  [the longest x4 13.4 us: project_side(): jnp.dot(inputs[layer], weights[layer], preferred_element_type=jnp.float32)]
    psum x1 -> x0, blocking collectives: 6.85 us -> none  [per_device(): scores = lax.psum(block, ('tensor', 'sub'))]
    unnamed x8 -> x2, local copies, waits for them, and re-layouts: 0.02 us -> 2.55 us
    concatenate x2 -> x0, other arithmetic: 1.69 us -> none  [project_side(): jnp.concatenate([jnp.dot(inputs[layer], weights[layer], preferred_element...]
  transfers between devices with their start and end apart: 2 -> 0, of which waited for: 1 -> 0; matrix products, arithmetic and copies ran while one was open for 3% -> 0% of each run, Pallas kernels for 0% -> 0%
where the time goes in v1:
time: 31.4 us; the launch traced here: 31.2 us
  Pallas kernels  28 us (89%)
  local copies, waits for them, and re-layouts  2.55 us (8%)
  between operations  0.64 us (2%)
    pallas_call x1, Pallas kernels, fused(): pl.pallas_call(functools.partial(kernel, dps, chunk, steps), out_shape=(j...  28 us
    unnamed x2, local copies, waits for them, and re-layouts  2.55 us

profile of v1, /device:TPU:0, one launch (start us, length us, event | category | flops | bytes accessed | tf_op | source)
XLA Modules:
  0.0 31.2 jit_solution(17177551860573261963)
XLA Ops:
  0.6 28.0 %shard_map.77 = (f32[2,2048]{1,0:T(2,128)}, f32[2,256]{1,0:T(2,128)}) custom-call(bf16[2,1024,3584]{2,1,0:T(8,128)(2,1)} %x_hbm.1, bf16[2,1024,1024]{2,1,0:T(8,128)(2,1)} %g_hbm.1, s32[2]{0:T(128)} %len_ref.1, bf16[2,64,3584]{2,1,0:T(8,128)(2,1)} %bitcast.3, bf16[2,64,1024]{2,1,0:T(8,128)(2,1)} %bitcast.4, bf16[64,2048]{1,0:T(8,128)(2,1)} %q_hbm.1), custom_call_target="tpu_custom_call" | custom-call | tf_op jit(solution)/shard_map/pallas_call | solution.py:266
  28.6 1.3 %copy.10 = f32[2,2048]{1,0:T(2,128)} copy(f32[2,2048]{1,0:T(2,128)} %get-tuple-element.8) | data formatting | bytes 32768
  29.9 1.2 %copy.11 = f32[256,2]{0,1:T(2,128)} copy(f32[256,2]{0,1:T(2,128)} %bitcast.5) | data formatting | bytes 4096

commit v2 on v1

--- a/solution.py
+++ b/solution.py
@@ -249,6 +249,11 @@
         sc_ref[:, dd * rows_q : (dd + 1) * rows_q] = acc[0:2, 0:rows_q]
     for copy in sub_copies + ten_copies + sk_copies + sc_copies:
         copy.wait_send()
+
+
+def hand_out(sk_in, sc_in, sk_out, sc_out):
+    sk_out[...] = sk_in[...]
+    sc_out[...] = sc_in[...]
 
 
 def fused(dps, acts, grads_out, lengths, proj_in, proj_out, query_grads):
@@ -295,6 +300,13 @@
             collective_id=0, has_side_effects=True, vmem_limit_bytes=60 * 1024 * 1024
         ),
     )(acts, grads_out, lengths, proj_in.swapaxes(1, 2), proj_out.swapaxes(1, 2), query_grads)
+    sketches, scores = pl.pallas_call(
+        hand_out,
+        out_shape=(
+            jax.ShapeDtypeStruct(sketches.shape, f32),
+            jax.ShapeDtypeStruct(scores.shape, f32),
+        ),
+    )(sketches, scores)
     return sketches, scores.T
 
 

time: 31.4 us -> 30.2 us (0.962)
  local copies, waits for them, and re-layouts: 2.55 us -> 0 us
  Pallas kernels: 28 us -> 29.3 us
    unnamed x2 -> x0, local copies, waits for them, and re-layouts: 2.55 us -> none
    pallas_call x0 -> x1, Pallas kernels: none -> 1.33 us  [fused(): pl.pallas_call(hand_out, out_shape=(jax.ShapeDtypeStruct(sketches.shape,...]
where the time goes in v2:
time: 30.2 us; the launch traced here: 29.9 us
  Pallas kernels  29.3 us (97%)
  between operations  0.64 us (2%)
    pallas_call x1, Pallas kernels, fused(): pl.pallas_call(functools.partial(kernel, dps, chunk, steps), out_shape=(j...  28 us
    pallas_call x1, Pallas kernels, fused(): pl.pallas_call(hand_out, out_shape=(jax.ShapeDtypeStruct(sketches.shape,...  1.33 us

profile of v2, /device:TPU:0, one launch (start us, length us, event | category | flops | bytes accessed | tf_op | source)
XLA Modules:
  0.0 29.9 jit_solution(2211501823727826874)
XLA Ops:
  0.6 28.0 %shard_map.77 = (f32[2,2048]{1,0:T(2,128)}, f32[2,256]{1,0:T(2,128)}) custom-call(bf16[2,1024,3584]{2,1,0:T(8,128)(2,1)} %x_hbm.1, bf16[2,1024,1024]{2,1,0:T(8,128)(2,1)} %g_hbm.1, s32[2]{0:T(128)} %len_ref.1, bf16[2,64,3584]{2,1,0:T(8,128)(2,1)} %bitcast.3, bf16[2,64,1024]{2,1,0:T(8,128)(2,1)} %bitcast.4, bf16[64,2048]{1,0:T(8,128)(2,1)} %q_hbm.1), custom_call_target="tpu_custom_call" | custom-call | tf_op jit(solution)/shard_map/pallas_call | solution.py:271
  28.6 1.3 %shard_map.78 = (f32[2,2048]{1,0:T(2,128)}, f32[2,256]{1,0:T(2,128)}) custom-call(f32[2,2048]{1,0:T(2,128)} %get-tuple-element.6.sk_in, f32[2,256]{1,0:T(2,128)} %get-tuple-element.7.sc_in), custom_call_target="tpu_custom_call" | custom-call | tf_op jit(solution)/shard_map/pallas_call | solution.py:303

commit v3 on v2

--- a/solution.py
+++ b/solution.py
@@ -102,15 +102,23 @@
 
     loads = []
     weight_loads = [fetch_w(0, ot), fetch_w(1, t)]
-    for n in range(len(items)):
+    q_load = pltpu.make_async_copy(q_hbm, q, q_sem)
+
+    def begin(n):
+        if n == len(items):
+            q_load.start()
+        if n >= len(items):
+            return
         if n == 0 or n == len(items) // 2:
             for copy in weight_loads[0 if n == 0 else 1]:
                 copy.start()
         loads.append(fetch(n))
         for copy in loads[-1]:
             copy.start()
-    q_load = pltpu.make_async_copy(q_hbm, q, q_sem)
-    q_load.start()
+
+    ahead = 2
+    for n in range(ahead):
+        begin(n)
 
     others = []
     for a in range(dps):
@@ -130,6 +138,7 @@
                 copy.wait()
         for copy in loads[n]:
             copy.wait()
+        begin(n + ahead)
         layer, row = items[n]
         at = pl.ds(pl.multiple_of(row, chunk), chunk)
         out[:, 0:k] = lax.dot_general(x[layer, at, :], w[layer], NT, preferred_element_type=jnp.float32)

time: 30.2 us -> 27.8 us (0.921)
  Pallas kernels: 29.3 us -> 27 us
    pallas_call x1, Pallas kernels: 28 us -> 25.6 us  [fused(): pl.pallas_call(functools.partial(kernel, dps, chunk, steps), out_shape=(j...]
where the time goes in v3:
time: 27.8 us; the launch traced here: 27.6 us
  Pallas kernels  27 us (97%)
  between operations  0.64 us (2%)
    pallas_call x1, Pallas kernels, fused(): pl.pallas_call(functools.partial(kernel, dps, chunk, steps), out_shape=(j...  25.6 us
    pallas_call x1, Pallas kernels, fused(): pl.pallas_call(hand_out, out_shape=(jax.ShapeDtypeStruct(sketches.shape,...  1.33 us

profile of v3, /device:TPU:0, one launch (start us, length us, event | category | flops | bytes accessed | tf_op | source)
XLA Modules:
  0.0 27.6 jit_solution(8645641592597488824)
XLA Ops:
  0.6 25.6 %shard_map.77 = (f32[2,2048]{1,0:T(2,128)}, f32[2,256]{1,0:T(2,128)}) custom-call(bf16[2,1024,3584]{2,1,0:T(8,128)(2,1)} %x_hbm.1, bf16[2,1024,1024]{2,1,0:T(8,128)(2,1)} %g_hbm.1, s32[2]{0:T(128)} %len_ref.1, bf16[2,64,3584]{2,1,0:T(8,128)(2,1)} %bitcast.3, bf16[2,64,1024]{2,1,0:T(8,128)(2,1)} %bitcast.4, bf16[64,2048]{1,0:T(8,128)(2,1)} %q_hbm.1), custom_call_target="tpu_custom_call" | custom-call | tf_op jit(solution)/shard_map/pallas_call | solution.py:280
  26.3 1.3 %shard_map.78 = (f32[2,2048]{1,0:T(2,128)}, f32[2,256]{1,0:T(2,128)}) custom-call(f32[2,2048]{1,0:T(2,128)} %get-tuple-element.6.sk_in, f32[2,256]{1,0:T(2,128)} %get-tuple-element.7.sc_in), custom_call_target="tpu_custom_call" | custom-call | tf_op jit(solution)/shard_map/pallas_call | solution.py:312
